TPU v7x, 32 devices: a whole 2x2x4 slice. The times are simulated.
32 devices in a mesh: pool: 16 (over z, y, core), tensor: 2 (over x).
Axes of the slice: x: 2, y: 2, z: 4, core: 2. Of those that a mesh axis runs over, the one named last changes fastest.
Arguments:
- queries: bfloat16 [2048, 4096], P(('pool', 'tensor')), may hold values from -6 to 6
- incoming_keys: bfloat16 [2048, 2048], P(('pool', 'tensor')), may hold values from -6 to 6
- incoming_values: bfloat16 [2048, 2048], P(('pool', 'tensor')), may hold values from -6 to 6
- cached_key_pages: bfloat16 [256, 128, 2048], P('pool', None, 'tensor'), may hold values from -6 to 6
- cached_value_pages: bfloat16 [256, 128, 2048], P('pool', None, 'tensor'), may hold values from -6 to 6
- page_table: int32 [16, 64], replicated, may hold values from -1 to 255, as said below
- lengths: int32 [16], replicated, may hold values from 1 to 8192, as said below
Outputs:
- attended: bfloat16 [2048, 4096], P(('pool', 'tensor'))
Inputs may be any that keep to these rules, and one draw needn't show every extreme that they name: Request r has ceil(lengths[r] / 128) pages; for j below that, page_table[r, j] is the slot of its page j, a slot g of pool device g // 16, which is one of r, r + 1, ..., r + 3 counted modulo 16. No slot holds two pages. All other entries are -1. `lengths`: some request has exactly 8192 cached tokens.
All inputs are finite; a program needn't handle non-finite values.
Results may differ from a plain program's by a relative error of at most 0.008.
Values may be sent and summed in bfloat16 or wider, within the bound.
A program may use at most 64 MiB of HBM per device.

v0:
```python
import jax
import jax.numpy as jnp
from jax import lax
from jax.sharding import PartitionSpec as P

QUERY_HEADS = 16
KEY_VALUE_HEADS = 8
HEAD_SIZE = 256
SPAN = 4


SOFTCAP = 50.0


def shifted(block, axis, distance):
    devices = range(lax.axis_size(axis))
    route = [((i - distance) % len(devices), i) for i in devices]
    return lax.ppermute(block, axis, route)


def capped(scores, visible):
    capped_scores = SOFTCAP * jnp.tanh(scores / SOFTCAP)
    return jnp.where(visible, jnp.exp(capped_scores), 0.0).astype(jnp.bfloat16)


def on_device(
    queries,
    incoming_keys,
    incoming_values,
    cached_key_pages,
    cached_value_pages,
    page_table,
    lengths,
):
    heads_q, keys_new, values_new = (
        lax.all_to_all(queries, "tensor", split_axis=1, concat_axis=0, tiled=True),
        lax.all_to_all(incoming_keys, "tensor", split_axis=1, concat_axis=0, tiled=True),
        lax.all_to_all(incoming_values, "tensor", split_axis=1, concat_axis=0, tiled=True),
    )
    stretch_len = heads_q.shape[0]
    kv_heads = keys_new.shape[1] // HEAD_SIZE
    query_group_width = QUERY_HEADS // KEY_VALUE_HEADS
    head_count = kv_heads * query_group_width
    score_scale = HEAD_SIZE ** (-0.5)
    query_layout_grid = heads_q.reshape(stretch_len, kv_heads, query_group_width, HEAD_SIZE)
    key_own = keys_new.reshape(stretch_len, kv_heads, HEAD_SIZE)
    value_own = values_new.reshape(stretch_len, kv_heads, HEAD_SIZE)
    causal = jnp.arange(stretch_len)[None, :] <= jnp.arange(stretch_len)[:, None]
    own_scores = (
        jnp.einsum("qgah,kgh->gaqk", query_layout_grid, key_own, preferred_element_type=jnp.float32)
        * score_scale
    )
    own_weights = capped(own_scores, causal)
    own_numer = jnp.einsum(
        "gaqk,kgh->qgah", own_weights, value_own, preferred_element_type=jnp.float32
    )
    own_numer = own_numer.reshape(stretch_len, head_count * HEAD_SIZE)
    own_total = jnp.transpose(jnp.sum(own_weights.astype(jnp.float32), axis=-1), (2, 0, 1)).reshape(
        stretch_len, head_count
    )
    received = [heads_q] + [shifted(heads_q, "pool", offset) for offset in range(1, SPAN)]
    stacked = jnp.stack(received)
    pool_size = lax.axis_size("pool")
    holder = lax.axis_index("pool")
    slots_dev = cached_key_pages.shape[0]
    page_len = cached_key_pages.shape[1]
    owners = (holder - jnp.arange(SPAN, dtype=jnp.int32)) % pool_size
    table_rows = jnp.take(page_table, owners, axis=0)
    global_slot = holder * slots_dev + jnp.arange(slots_dev, dtype=jnp.int32)
    matches = table_rows[:, :, None] == global_slot[None, None, :]
    owner_hot = jnp.any(matches, axis=1)
    page_index = jnp.sum(
        jnp.where(matches, jnp.arange(table_rows.shape[1], dtype=jnp.int32)[None, :, None], 0),
        axis=(0, 1),
    )
    distance = jnp.sum(jnp.where(owner_hot, jnp.arange(SPAN, dtype=jnp.int32)[:, None], 0), axis=0)
    alive_slot = jnp.any(owner_hot, axis=0)
    owner_len = jnp.take(lengths, owners)
    slot_len = jnp.sum(jnp.where(owner_hot, owner_len[:, None], 0), axis=0)
    group_pages = 4
    group_count = slots_dev // group_pages

    def compute(running, input_arrays):
        (
            key_page_block,
            value_page_block,
            picks,
            index_block,
            limit_block,
            alive_block,
            hot_block,
        ) = input_arrays
        query_pick = jnp.take(stacked, picks, axis=0).reshape(
            group_pages, stretch_len, kv_heads, query_group_width, HEAD_SIZE
        )
        key_layout_grid = key_page_block.reshape(group_pages, page_len, kv_heads, HEAD_SIZE)
        value_layout_grid = value_page_block.reshape(group_pages, page_len, kv_heads, HEAD_SIZE)
        scores = (
            jnp.einsum(
                "pqgah,pkgh->pgaqk", query_pick, key_layout_grid, preferred_element_type=jnp.float32
            )
            * score_scale
        )
        position = index_block[:, None] * page_len + jnp.arange(page_len, dtype=jnp.int32)[None, :]
        visible = position < limit_block[:, None]
        weights = capped(scores, visible[:, None, None, None, :])
        numerator = jnp.einsum(
            "pgaqk,pkgh->pqgah", weights, value_layout_grid, preferred_element_type=jnp.float32
        )
        numerator = numerator.reshape(group_pages, stretch_len, head_count * HEAD_SIZE)
        totals = jnp.sum(weights.astype(jnp.float32), axis=-1)
        totals = jnp.transpose(totals, (0, 3, 1, 2)).reshape(group_pages, stretch_len, head_count)
        numer_acc, total_acc = running
        numer_acc = numer_acc + jnp.einsum(
            "pd,pqx->dqx", hot_block, numerator, precision=lax.Precision.HIGHEST
        )
        total_acc = total_acc + jnp.einsum(
            "pd,pqx->dqx", hot_block, totals, precision=lax.Precision.HIGHEST
        )
        return (numer_acc, total_acc)

    def one_group(running, input_arrays):
        running = compute(running, input_arrays)
        return (running, None)

    start_offset = (
        jnp.zeros((SPAN, stretch_len, head_count * HEAD_SIZE), jnp.float32),
        jnp.zeros((SPAN, stretch_len, head_count), jnp.float32),
    )
    input_arrays = (
        cached_key_pages.reshape(group_count, group_pages, page_len, kv_heads * HEAD_SIZE),
        cached_value_pages.reshape(group_count, group_pages, page_len, kv_heads * HEAD_SIZE),
        distance.reshape(group_count, group_pages),
        page_index.reshape(group_count, group_pages),
        slot_len.reshape(group_count, group_pages),
        alive_slot.reshape(group_count, group_pages),
        jnp.transpose(owner_hot).astype(jnp.float32).reshape(group_count, group_pages, SPAN),
    )
    (numer_acc, total_acc), _ = lax.scan(one_group, start_offset, input_arrays)
    numerator = numer_acc[0]
    totals = total_acc[0]
    for offset in range(1, SPAN):
        recv_numer, recv_total = shifted((numer_acc[offset], total_acc[offset]), "pool", -offset)
        numerator = numerator + recv_numer
        totals = totals + recv_total
    numerator = numerator + own_numer
    totals = totals + own_total
    attended = numerator.reshape(stretch_len, head_count, HEAD_SIZE) / totals[:, :, None]
    attended = attended.reshape(stretch_len, head_count * HEAD_SIZE).astype(jnp.bfloat16)
    return lax.all_to_all(attended, "tensor", split_axis=0, concat_axis=1, tiled=True)


def solution(mesh):
    placed = (
        P(("pool", "tensor"), None),
        P(("pool", "tensor"), None),
        P(("pool", "tensor"), None),
        P("pool", None, "tensor"),
        P("pool", None, "tensor"),
        P(),
        P(),
    )
    return jax.shard_map(
        on_device,
        mesh=mesh,
        in_specs=placed,
        out_specs=P(("pool", "tensor"), None),
        check_vma=False,
    )
```

profile of v0, /device:TPU:0, one launch (start us, length us, event | category | flops | bytes accessed | tf_op | source)
XLA Modules:
  0.0 256.3 jit_solution(11782580924899864981)
XLA Ops:
  1.9 4.2 %all-to-all-start = ((bf16[64,2,2048]{2,0,1:T(8,128)(2,1)}), bf16[64,2,2048]{2,0,1:T(8,128)(2,1)S(1)}, u32[]{:S(2)}, u32[]{:S(2)}) async-start(bf16[64,2,2048]{2,0,1:T(8,128)(2,1)} %bitcast.130), calls=%async_computation | async-start | bytes 1048576 | tf_op jit(solution)/shard_map/all_to_all | solution.py:36
  8.3 6.6 %all-to-all-done = bf16[64,2,2048]{2,0,1:T(8,128)(2,1)S(1)} async-done(((bf16[64,2,2048]{2,0,1:T(8,128)(2,1)}), bf16[64,2,2048]{2,0,1:T(8,128)(2,1)S(1)}, u32[]{:S(2)}, u32[]{:S(2)}) %all-to-all-start) | async-done | bytes 524320 | tf_op jit(solution)/shard_map/all_to_all | solution.py:36
  14.9 3.4 %all-to-all-start.1 = ((bf16[64,2,1024]{2,0,1:T(8,128)(2,1)}), bf16[64,2,1024]{2,0,1:T(8,128)(2,1)S(1)}, u32[]{:S(2)}, u32[]{:S(2)}) async-start(bf16[64,2,1024]{2,0,1:T(8,128)(2,1)} %bitcast.132), calls=%async_computation.1 | async-start | bytes 524288 | tf_op jit(solution)/shard_map/all_to_all | solution.py:37
  22.7 6.4 %copy.135 = bf16[16,128,1024]{1,2,0:T(8,128)(2,1)} copy(bf16[16,128,1024]{2,1,0:T(8,128)(2,1)} %param.13) | data formatting | bytes 8388608 | tf_op args[4]
  29.1 6.5 %copy.136 = bf16[16,128,1024]{1,2,0:T(8,128)(2,1)} copy(bf16[16,128,1024]{2,1,0:T(8,128)(2,1)} %param.12) | data formatting | bytes 8388608 | tf_op args[3]
  36.2 5.4 %collective-permute-done.2 = bf16[128,2048]{1,0:T(8,128)(2,1)S(1)} collective-permute-done((bf16[128,2048]{1,0:T(8,128)(2,1)S(1)}, bf16[128,2048]{1,0:T(8,128)(2,1)S(1)}, u32[]{:S(2)}, u32[]{:S(2)}) %collective-permute-start.2) | collective-permute-done | bytes 524320 | tf_op jit(solution)/shard_map/ppermute | solution.py:18
  41.7 9.4 %collective-permute-done = bf16[128,2048]{1,0:T(8,128)(2,1)S(1)} collective-permute-done((bf16[128,2048]{1,0:T(8,128)(2,1)S(1)}, bf16[128,2048]{1,0:T(8,128)(2,1)S(1)}, u32[]{:S(2)}, u32[]{:S(2)}) %collective-permute-start) | collective-permute-done | bytes 524320 | tf_op jit(solution)/shard_map/ppermute | solution.py:18
  52.7 116.8 %while.15 = (s32[]{:T(128)}, f32[4,128,2048]{2,0,1:T(4,128)}, f32[4,128,8]{1,0,2:T(4,128)S(1)}, f32[4,4,4]{2,1,0:T(4,128)S(1)}, bf16[4,4,128,1024]{2,3,1,0:T(8,1...) while((s32[]{:T(128)}, f32[4,128,2048]{2,0,1:T(4,128)}, ...), condition=%wide.region_6.7_spmd.clone, body=%wide.region_4.6_spmd.clone.sunk | while | flops 593696768 | bytes 52503912 | solution.py:139
  55.1 2.8 %gather.30 = bf16[4,128,4,2,256]{4,3,2,1,0:T(2,128)(2,1)} reshape(bf16[4,128,2048]{2,1,0:T(8,128)(2,1)S(1)} %gather_fusion) | data formatting | bytes 4194304 | tf_op jit(solution)/shard_map/while/body/eval_jaxpr/jit(_take)/gather | solution.py:93
  64.3 5.5 %copy.207 = f32[4,128,2048]{2,0,1:T(4,128)} copy(f32[4,128,2048]{1,2,0:T(8,128)} %bitcast.161) | data formatting | bytes 8388608 | tf_op jit(solution)/shard_map/while/body/eval_jaxpr/reshape | solution.py:110
  69.7 11.7 %select_add_fusion.2 = f32[4,128,2048]{2,0,1:T(4,128)} fusion(f32[4,128,2048]{2,0,1:T(4,128)} %get-tuple-element.347, f32[4,128,2048]{2,0,1:T(4,128)} %copy.207, pred[]{:T(512)S(6)} %compare.13, f32[4,4,4]{2,1,0:T(4,128)S(1)} %get-tuple-element.361, s32[]{:T(128)} %get-tuple-element.346), kind=kOutput, calls=%fused_computation.3.clone.2 | convolution fusion | flops 52428800 | bytes 12584965 | tf_op jit(solution)/shard_map/while/body/eval_jaxpr/pd,pqx->dqx/dot_general | solution.py:114
  93.2 5.5 %copy.207 = f32[4,128,2048]{2,0,1:T(4,128)} copy(f32[4,128,2048]{1,2,0:T(8,128)} %bitcast.161) | data formatting | bytes 8388608 | tf_op jit(solution)/shard_map/while/body/eval_jaxpr/reshape | solution.py:110
  98.7 12.0 %select_add_fusion.2 = f32[4,128,2048]{2,0,1:T(4,128)} fusion(f32[4,128,2048]{2,0,1:T(4,128)} %get-tuple-element.347, f32[4,128,2048]{2,0,1:T(4,128)} %copy.207, pred[]{:T(512)S(6)} %compare.13, f32[4,4,4]{2,1,0:T(4,128)S(1)} %get-tuple-element.361, s32[]{:T(128)} %get-tuple-element.346), kind=kOutput, calls=%fused_computation.3.clone.2 | convolution fusion | flops 52428800 | bytes 12584965 | tf_op jit(solution)/shard_map/while/body/eval_jaxpr/pd,pqx->dqx/dot_general | solution.py:114
  113.3 2.8 %gather.30 = bf16[4,128,4,2,256]{4,3,2,1,0:T(2,128)(2,1)} reshape(bf16[4,128,2048]{2,1,0:T(8,128)(2,1)S(1)} %gather_fusion) | data formatting | bytes 4194304 | tf_op jit(solution)/shard_map/while/body/eval_jaxpr/jit(_take)/gather | solution.py:93
  122.5 5.5 %copy.207 = f32[4,128,2048]{2,0,1:T(4,128)} copy(f32[4,128,2048]{1,2,0:T(8,128)} %bitcast.161) | data formatting | bytes 8388608 | tf_op jit(solution)/shard_map/while/body/eval_jaxpr/reshape | solution.py:110
  128.0 12.0 %select_add_fusion.2 = f32[4,128,2048]{2,0,1:T(4,128)} fusion(f32[4,128,2048]{2,0,1:T(4,128)} %get-tuple-element.347, f32[4,128,2048]{2,0,1:T(4,128)} %copy.207, pred[]{:T(512)S(6)} %compare.13, f32[4,4,4]{2,1,0:T(4,128)S(1)} %get-tuple-element.361, s32[]{:T(128)} %get-tuple-element.346), kind=kOutput, calls=%fused_computation.3.clone.2 | convolution fusion | flops 52428800 | bytes 12584965 | tf_op jit(solution)/shard_map/while/body/eval_jaxpr/pd,pqx->dqx/dot_general | solution.py:114
  142.6 2.8 %gather.30 = bf16[4,128,4,2,256]{4,3,2,1,0:T(2,128)(2,1)} reshape(bf16[4,128,2048]{2,1,0:T(8,128)(2,1)S(1)} %gather_fusion) | data formatting | bytes 4194304 | tf_op jit(solution)/shard_map/while/body/eval_jaxpr/jit(_take)/gather | solution.py:93
  151.8 5.5 %copy.207 = f32[4,128,2048]{2,0,1:T(4,128)} copy(f32[4,128,2048]{1,2,0:T(8,128)} %bitcast.161) | data formatting | bytes 8388608 | tf_op jit(solution)/shard_map/while/body/eval_jaxpr/reshape | solution.py:110
  157.3 12.0 %select_add_fusion.2 = f32[4,128,2048]{2,0,1:T(4,128)} fusion(f32[4,128,2048]{2,0,1:T(4,128)} %get-tuple-element.347, f32[4,128,2048]{2,0,1:T(4,128)} %copy.207, pred[]{:T(512)S(6)} %compare.13, f32[4,4,4]{2,1,0:T(4,128)S(1)} %get-tuple-element.361, s32[]{:T(128)} %get-tuple-element.346), kind=kOutput, calls=%fused_computation.3.clone.2 | convolution fusion | flops 52428800 | bytes 12584965 | tf_op jit(solution)/shard_map/while/body/eval_jaxpr/pd,pqx->dqx/dot_general | solution.py:114
  169.5 5.3 %copy.139 = f32[4,128,2048]{1,2,0:T(8,128)} copy(f32[4,128,2048]{2,0,1:T(4,128)} %get-tuple-element.131) | data formatting | bytes 8388608 | tf_op jit(solution)/shard_map/while | solution.py:139
  174.8 3.4 %all-to-all-start.2 = ((bf16[64,2,1024]{2,0,1:T(8,128)(2,1)}), bf16[64,2,1024]{2,0,1:T(8,128)(2,1)S(1)}, u32[]{:S(2)}, u32[]{:S(2)}) async-start(bf16[64,2,1024]{2,0,1:T(8,128)(2,1)} %bitcast.131), calls=%async_computation.2 | async-start | bytes 524288 | tf_op jit(solution)/shard_map/all_to_all | solution.py:38
  178.3 3.6 %slice_bitcast_fusion.2 = (f32[128,2048]{0,1:T(8,128)}, f32[128,2048]{0,1:T(8,128)}, f32[128,2048]{0,1:T(8,128)}) fusion(f32[4,128,2048]{1,2,0:T(8,128)} %copy.139), kind=kLoop, calls=%fused_computation.45 | loop fusion | bytes 6291456 | tf_op jit(solution)/shard_map/squeeze | solution.py:143
  186.6 52.7 %collective-permute-done.7 = f32[128,8]{0,1:T(8,128)S(1)} collective-permute-done((f32[128,8]{0,1:T(8,128)S(1)}, f32[128,8]{0,1:T(8,128)S(1)}, u32[]{:S(2)}, u32[]{:S(2)}) %collective-permute-start.7) | collective-permute-done | bytes 4128 | tf_op jit(solution)/shard_map/ppermute | solution.py:18
  243.4 12.1 %all_to_all.70 = bf16[2,64,2048]{2,1,0:T(8,128)(2,1)S(1)} all-to-all(bf16[2,64,2048]{2,1,0:T(8,128)(2,1)S(1)} %bitcast.171), channel_id=1, replica_groups=mesh['pool'=16,'tensor'=2] {'tensor'}, dimensions={0} | all-to-all | bytes 1048576 | tf_op jit(solution)/shard_map/all_to_all | solution.py:150
  (110 shorter events, 58.9 us)
Async XLA Ops:
  0.0 6.9 %copy-start = (s32[16,64]{1,0:T(8,128)S(1)}, s32[16,64]{1,0:T(8,128)}, u32[]{:S(2)}) copy-start(s32[16,64]{1,0:T(8,128)} %param.14) | copy-start | bytes 12292
  0.0 6.2 %copy-start.1 = (s32[16]{0:T(128)S(1)}, s32[16]{0:T(128)}, u32[]{:S(2)}) copy-start(s32[16]{0:T(128)} %param.15) | copy-start | bytes 196
  0.0 7.5 %copy-start.3 = (bf16[64,2048]{1,0:T(8,128)(2,1)S(1)}, bf16[64,2048]{1,0:T(8,128)(2,1)}, u32[]{:S(2)}) copy-start(bf16[64,2048]{1,0:T(8,128)(2,1)} %param.10) | copy-start | bytes 786436
  1.9 12.9 %all-to-all-start = ((bf16[64,2,2048]{2,0,1:T(8,128)(2,1)}), bf16[64,2,2048]{2,0,1:T(8,128)(2,1)S(1)}, u32[]{:S(2)}, u32[]{:S(2)}) async-start(bf16[64,2,2048]{2,0,1:T(8,128)(2,1)} %bitcast.130), calls=%async_computation | async-start | bytes 1048576 | tf_op jit(solution)/shard_map/all_to_all | solution.py:36
  14.9 160.0 %all-to-all-start.1 = ((bf16[64,2,1024]{2,0,1:T(8,128)(2,1)}), bf16[64,2,1024]{2,0,1:T(8,128)(2,1)S(1)}, u32[]{:S(2)}, u32[]{:S(2)}) async-start(bf16[64,2,1024]{2,0,1:T(8,128)(2,1)} %bitcast.132), calls=%async_computation.1 | async-start | bytes 524288 | tf_op jit(solution)/shard_map/all_to_all | solution.py:37
  18.3 17.9 %collective-permute-start.1 = (bf16[128,2048]{1,0:T(8,128)(2,1)S(1)}, bf16[128,2048]{1,0:T(8,128)(2,1)S(1)}, u32[]{:S(2)}, u32[]{:S(2)}) collective-permute-start(bf16[128,2048]{1,0:T(8,128)(2,1)S(1)} %bitcast.166), channel_id=1, source_target_pairs={{28,0},{30,2},{0,4},{2,6},{4,8},{6,10},{8,12},{10,14},{12,16},{14,... | collective-permute-start | bytes 1572872 | tf_op jit(solution)/shard_map/ppermute | solution.py:18
  20.1 21.5 %collective-permute-start.2 = (bf16[128,2048]{1,0:T(8,128)(2,1)S(1)}, bf16[128,2048]{1,0:T(8,128)(2,1)S(1)}, u32[]{:S(2)}, u32[]{:S(2)}) collective-permute-start(bf16[128,2048]{1,0:T(8,128)(2,1)S(1)} %bitcast.167), channel_id=1, source_target_pairs={{26,0},{28,2},{30,4},{0,6},{2,8},{4,10},{6,12},{8,14},{10,16},{12,... | collective-permute-start | bytes 1572872 | tf_op jit(solution)/shard_map/ppermute | solution.py:18
  20.1 30.9 %collective-permute-start = (bf16[128,2048]{1,0:T(8,128)(2,1)S(1)}, bf16[128,2048]{1,0:T(8,128)(2,1)S(1)}, u32[]{:S(2)}, u32[]{:S(2)}) collective-permute-start(bf16[128,2048]{1,0:T(8,128)(2,1)S(1)} %bitcast.168), channel_id=1, source_target_pairs={{30,0},{0,2},{2,4},{4,6},{6,8},{8,10},{10,12},{12,14},{14,16},{16,... | collective-permute-start | bytes 1572872 | tf_op jit(solution)/shard_map/ppermute | solution.py:18
  29.1 6.5 %copy-start.4 = (bf16[64,2048]{1,0:T(8,128)(2,1)S(1)}, bf16[64,2048]{1,0:T(8,128)(2,1)}, u32[]{:S(2)}) copy-start(bf16[64,2048]{1,0:T(8,128)(2,1)} %param.11) | copy-start | bytes 786436
  57.9 2.2 copy-start.2
  86.8 2.2 copy-start.2
  116.1 2.2 copy-start.2
  145.4 2.2 copy-start.2
  174.8 9.0 %all-to-all-start.2 = ((bf16[64,2,1024]{2,0,1:T(8,128)(2,1)}), bf16[64,2,1024]{2,0,1:T(8,128)(2,1)S(1)}, u32[]{:S(2)}, u32[]{:S(2)}) async-start(bf16[64,2,1024]{2,0,1:T(8,128)(2,1)} %bitcast.131), calls=%async_computation.2 | async-start | bytes 524288 | tf_op jit(solution)/shard_map/all_to_all | solution.py:38
  181.9 58.8 %collective-permute-start.3 = (f32[128,2048]{0,1:T(8,128)}, f32[128,2048]{0,1:T(8,128)}, u32[]{:S(2)}, u32[]{:S(2)}) collective-permute-start(f32[128,2048]{0,1:T(8,128)} %get-tuple-element.254), channel_id=1, source_target_pairs={{2,0},{4,2},{6,4},{8,6},{10,8},{12,10},{14,12},{16,14},{18,16},{20... | collective-permute-start | bytes 3145736 | tf_op jit(solution)/shard_map/ppermute | solution.py:18
  181.9 58.8 %collective-permute-start.4 = (f32[128,2048]{0,1:T(8,128)}, f32[128,2048]{0,1:T(8,128)}, u32[]{:S(2)}, u32[]{:S(2)}) collective-permute-start(f32[128,2048]{0,1:T(8,128)} %get-tuple-element.256), channel_id=1, source_target_pairs={{4,0},{6,2},{8,4},{10,6},{12,8},{14,10},{16,12},{18,14},{20,16},{2... | collective-permute-start | bytes 3145736 | tf_op jit(solution)/shard_map/ppermute | solution.py:18
  181.9 58.8 %collective-permute-start.5 = (f32[128,2048]{0,1:T(8,128)}, f32[128,2048]{0,1:T(8,128)}, u32[]{:S(2)}, u32[]{:S(2)}) collective-permute-start(f32[128,2048]{0,1:T(8,128)} %get-tuple-element.255), channel_id=1, source_target_pairs={{6,0},{8,2},{10,4},{12,6},{14,8},{16,10},{18,12},{20,14},{22,16},{... | collective-permute-start | bytes 3145736 | tf_op jit(solution)/shard_map/ppermute | solution.py:18
  184.5 54.9 %collective-permute-start.7 = (f32[128,8]{0,1:T(8,128)S(1)}, f32[128,8]{0,1:T(8,128)S(1)}, u32[]{:S(2)}, u32[]{:S(2)}) collective-permute-start(f32[128,8]{0,1:T(8,128)S(1)} %get-tuple-element.257), channel_id=1, source_target_pairs={{4,0},{6,2},{8,4},{10,6},{12,8},{14,10},{16,12},{18,14},{20,16},{2... | collective-permute-start | bytes 12296 | tf_op jit(solution)/shard_map/ppermute | solution.py:18
  186.6 53.5 %collective-permute-start.8 = (f32[128,8]{0,1:T(8,128)S(1)}, f32[128,8]{0,1:T(8,128)S(1)}, u32[]{:S(2)}, u32[]{:S(2)}) collective-permute-start(f32[128,8]{0,1:T(8,128)S(1)} %get-tuple-element.258), channel_id=1, source_target_pairs={{6,0},{8,2},{10,4},{12,6},{14,8},{16,10},{18,12},{20,14},{22,16},{... | collective-permute-start | bytes 12296 | tf_op jit(solution)/shard_map/ppermute | solution.py:18
  239.4 1.3 collective-permute-start.6
where the time goes:
time: 257 us; the launch traced here: 256 us
  local copies, waits for them, and re-layouts  79.7 us (31%)
  waiting for transfers between devices  74.8 us (29%)
  matrix products  66 us (26%)
  starting transfers between devices  18.2 us (7%)
  blocking collectives  12.1 us (5%)
  other arithmetic  5.12 us (2%)
    ppermute x9, waiting for transfers between devices, shifted(): return lax.ppermute(block, axis, route)  68.2 us
    dot_general x4, matrix products, compute(): jnp.einsum('pd,pqx->dqx', hot_block, numerator, precision=lax.Precision.H...  47.6 us
    reshape x4, local copies, waits for them, and re-layouts, compute(): numerator.reshape(group_pages, stretch_len, head_count * HEAD_SIZE)  21.9 us
    gather x8, local copies, waits for them, and re-layouts, compute(): jnp.take(stacked, picks, axis=0)  20.3 us
    unnamed x11, local copies, waits for them, and re-layouts  13 us
    all_to_all x1, blocking collectives, on_device(): lax.all_to_all(attended, 'tensor', split_axis=0, concat_axis=1, tiled=True)  12.1 us
    dot_general x4, matrix products, compute(): jnp.einsum('pgaqk,pkgh->pqgah', weights, value_layout_grid, preferred_ele...  10.6 us
    dynamic_slice x4, local copies, waits for them, and re-layouts, on_device(): (numer_acc, total_acc), _ = lax.scan(one_group, start_offset, input_arrays)  7.34 us
  transfers between devices with their start and end apart: 12, of which 5 were waited for; matrix products, arithmetic and copies ran while one was open for 56% of the time, Pallas kernels for 0%

commit v1 on v0

v1 whole, which is shorter than its diff:
```python
import functools
import math

import jax
import jax.numpy as jnp
from jax import lax
from jax.experimental import pallas as pl
from jax.experimental.pallas import tpu as pltpu
from jax.sharding import PartitionSpec as P

QUERY_HEADS = 16
KEY_VALUE_HEADS = 8
HEAD_SIZE = 256
SPAN = 4
SOFTCAP = 50.0

GROUP = QUERY_HEADS // KEY_VALUE_HEADS
WIDE = GROUP * HEAD_SIZE
INNER = HEAD_SIZE ** (-0.5) / SOFTCAP
OUTER = SOFTCAP * math.log2(math.e)
MESH = pl.DeviceIdType.MESH


def rows_by_head(block):
    return jnp.concatenate(
        [block[:, g * HEAD_SIZE : (g + 1) * HEAD_SIZE] for g in range(GROUP)], axis=0
    )


def tokens_by_head(block):
    n = block.shape[0] // GROUP
    return jnp.concatenate([block[g * n : (g + 1) * n] for g in range(GROUP)], axis=1)


def weigh(query, key):
    dots = lax.dot_general(query, key, (((1,), (1,)), ((), ())), preferred_element_type=jnp.float32)
    return jnp.exp2(OUTER * jnp.tanh(dots * INNER))


def kernel(
    n_pool,
    n_tensor,
    heads,
    dist,
    mask_rows,
    mask_each,
    q_in,
    k_in,
    v_in,
    k_pages,
    v_pages,
    out,
    *scratch,
):
    qbufs = scratch[:heads]
    (
        k_own,
        v_own,
        k_mem,
        v_mem,
        weights,
        own_numer,
        own_total,
        numer_out,
        total_out,
        numer_in,
        total_in,
        done,
        page_sem,
        local_sem,
        qx_send,
        qx_recv,
        kx_send,
        kx_recv,
        qf_send,
        qf_recv,
        nr_send,
        nr_recv,
        tr_send,
        tr_recv,
        ox_send,
        ox_recv,
    ) = scratch[heads:]
    p = lax.axis_index("pool")
    t = lax.axis_index("tensor")
    rows = q_in.shape[0]
    tokens = rows * n_tensor
    slots = k_pages.shape[0]
    page = k_pages.shape[1]
    span_cols = heads * HEAD_SIZE

    def pool_at(d):
        return (lax.rem(p + d + n_pool, n_pool), t)

    def tensor_at(i):
        return lax.rem(t + i, n_tensor)

    page_copies = []
    for h in range(heads):
        cols = slice(h * HEAD_SIZE, (h + 1) * HEAD_SIZE)
        page_copies.append(
            [
                pltpu.make_async_copy(k_pages.at[:, :, cols], k_mem.at[h], page_sem.at[h, 0]),
                pltpu.make_async_copy(v_pages.at[:, :, cols], v_mem.at[h], page_sem.at[h, 1]),
            ]
        )

    my_rows = pl.ds(pl.multiple_of(t * rows, rows), rows)

    def q_cols(owner, h):
        return pl.ds(pl.multiple_of((owner * heads + h) * WIDE, WIDE), WIDE)

    local = []
    for h in range(heads):
        local.append(
            pltpu.make_async_copy(
                q_in.at[:, q_cols(t, h)], qbufs[h].at[0, my_rows, :], local_sem.at[h]
            )
        )
    own_cols = pl.ds(pl.multiple_of(t * span_cols, span_cols), span_cols)
    local_kv = [
        pltpu.make_async_copy(k_in.at[:, own_cols], k_own.at[my_rows, :], local_sem.at[heads]),
        pltpu.make_async_copy(v_in.at[:, own_cols], v_own.at[my_rows, :], local_sem.at[heads + 1]),
    ]
    for c in local:
        c.start()
    for c in page_copies[0]:
        c.start()

    barrier = pltpu.get_barrier_semaphore()
    for i in range(1, n_tensor):
        pl.semaphore_signal(barrier, inc=1, device_id=(p, tensor_at(i)), device_id_type=MESH)
    for d in range(1, SPAN):
        pl.semaphore_signal(barrier, inc=1, device_id=pool_at(d), device_id_type=MESH)
        pl.semaphore_signal(barrier, inc=1, device_id=pool_at(-d), device_id_type=MESH)
    pl.semaphore_wait(barrier, n_tensor - 1 + 2 * (SPAN - 1))

    def remote(src, dst, send, recv, device):
        return pltpu.make_async_remote_copy(
            src_ref=src,
            dst_ref=dst,
            send_sem=send,
            recv_sem=recv,
            device_id=device,
            device_id_type=MESH,
        )

    exchange = []
    for h in range(heads):
        exchange.append(
            [
                remote(
                    q_in.at[:, q_cols(tensor_at(i), h)],
                    qbufs[h].at[0, my_rows, :],
                    qx_send.at[h, i],
                    qx_recv.at[h, i],
                    (p, tensor_at(i)),
                )
                for i in range(1, n_tensor)
            ]
        )
        for c in exchange[h]:
            c.start()
    exchange_kv = []
    for i in range(1, n_tensor):
        their_cols = pl.ds(pl.multiple_of(tensor_at(i) * span_cols, span_cols), span_cols)
        for j, (src, dst) in enumerate(((k_in, k_own), (v_in, v_own))):
            exchange_kv.append(
                remote(
                    src.at[:, their_cols],
                    dst.at[my_rows, :],
                    kx_send.at[j, i],
                    kx_recv.at[j, i],
                    (p, tensor_at(i)),
                )
            )
    for c in local_kv:
        c.start()
    for c in exchange_kv:
        c.start()
    for pair in page_copies[1:]:
        for c in pair:
            c.start()

    forward = []
    for h in range(heads):
        local[h].wait()
        for c in exchange[h]:
            c.wait_recv()
        forward.append(
            [
                remote(
                    qbufs[h].at[0],
                    qbufs[h].at[d],
                    qf_send.at[h, d],
                    qf_recv.at[h, d],
                    pool_at(d),
                )
                for d in range(1, SPAN)
            ]
        )
        for c in forward[h]:
            c.start()

    back = []
    for h in range(heads):
        for c in page_copies[h]:
            c.wait()
        for c in forward[h]:
            c.wait_recv()

        qbuf = qbufs[h]

        @pl.loop(0, slots // 4)
        def _(j):
            for u in range(4):
                s = j * 4 + u
                query = rows_by_head(qbuf[dist[s]])
                cols = pl.ds(pl.multiple_of(s * page, page), page)
                weights[:, cols] = weigh(query, k_mem[h, s]).astype(jnp.bfloat16)

        values = v_mem[h].reshape(slots * page, HEAD_SIZE)
        totals = lax.dot_general(
            mask_rows[...],
            weights[...],
            (((1,), (1,)), ((), ())),
            preferred_element_type=jnp.float32,
        )
        own_total[h] = totals
        total_out[h] = totals
        back.append([])
        for d in list(range(1, SPAN)) + [0]:
            all_weights = weights[...]
            kept = all_weights.reshape(-1, 16, slots * page) * mask_each[d][None]
            numer = jnp.dot(
                kept.reshape(all_weights.shape), values, preferred_element_type=jnp.float32
            )
            if d == 0:
                own_numer[h] = numer
            else:
                numer_out[h, d - 1] = tokens_by_head(numer.astype(jnp.bfloat16))
                pair = [
                    remote(
                        numer_out.at[h, d - 1],
                        numer_in.at[h, d - 1],
                        nr_send.at[h, d],
                        nr_recv.at[h, d],
                        pool_at(-d),
                    ),
                    remote(
                        total_out.at[h],
                        total_in.at[h, d - 1],
                        tr_send.at[h, d],
                        tr_recv.at[h, d],
                        pool_at(-d),
                    ),
                ]
                for c in pair:
                    c.start()
                back[h] += pair

    for c in local_kv:
        c.wait()
    for c in exchange_kv:
        c.wait_recv()
    n_rows = GROUP * tokens
    query_token = lax.broadcasted_iota(jnp.int32, (n_rows, tokens), 0) % tokens
    causal = lax.broadcasted_iota(jnp.int32, (n_rows, tokens), 1) <= query_token
    ones = jnp.ones((16, tokens), jnp.bfloat16)
    for h in range(heads):
        cols = slice(h * HEAD_SIZE, (h + 1) * HEAD_SIZE)
        fresh = jnp.where(causal, weigh(rows_by_head(qbufs[h][0]), k_own[:, cols]), 0.0)
        fresh = fresh.astype(jnp.bfloat16)
        own_numer[h] += jnp.dot(fresh, v_own[:, cols], preferred_element_type=jnp.float32)
        own_total[h] += lax.dot_general(
            ones, fresh, (((1,), (1,)), ((), ())), preferred_element_type=jnp.float32
        )

    finished = []
    for h in range(heads):
        for c in back[h]:
            c.wait_recv()
        total = own_total[h, 0:1, :]
        numer = own_numer[h]
        for d in range(1, SPAN):
            total = total + total_in[h, d - 1, d : d + 1, :]
            numer = numer + rows_by_head(numer_in[h, d - 1].astype(jnp.float32))
        per_row = jnp.broadcast_to(total, (128, n_rows)).T
        per_row = jnp.concatenate([per_row] * (HEAD_SIZE // 128), axis=1)
        done[h] = tokens_by_head((numer / per_row).astype(jnp.bfloat16))
        mine = pltpu.make_async_copy(
            done.at[h, my_rows, :], out.at[:, q_cols(t, h)], local_sem.at[heads + 2 + h]
        )
        mine.start()
        finished.append([mine])
        for i in range(1, n_tensor):
            their_rows = pl.ds(pl.multiple_of(tensor_at(i) * rows, rows), rows)
            c = remote(
                done.at[h, their_rows, :],
                out.at[:, q_cols(t, h)],
                ox_send.at[h, i],
                ox_recv.at[h, i],
                (p, tensor_at(i)),
            )
            c.start()
            finished[h].append(c)

    for h in range(heads):
        for c in exchange[h] + forward[h] + back[h]:
            c.wait_send()
        for c in finished[h]:
            c.wait()
    for c in exchange_kv:
        c.wait_send()


def on_device(
    n_pool, n_tensor, queries, incoming_keys, incoming_values, k_pages, v_pages, page_table, lengths
):
    slots, page, cols = k_pages.shape
    heads = cols // HEAD_SIZE
    rows = queries.shape[0]
    tokens = rows * n_tensor
    holder = lax.axis_index("pool")
    owners = (holder - jnp.arange(SPAN, dtype=jnp.int32)) % n_pool
    table_rows = jnp.take(page_table, owners, axis=0)
    global_slot = holder * slots + jnp.arange(slots, dtype=jnp.int32)
    matches = table_rows[:, :, None] == global_slot[None, None, :]
    page_index = jnp.arange(table_rows.shape[1], dtype=jnp.int32)[None, :, None]
    seen = jnp.sum(
        jnp.where(matches, jnp.take(lengths, owners)[:, None, None] - page_index * page, 0), axis=1
    )
    distance = jnp.sum(
        jnp.where(jnp.any(matches, axis=1), jnp.arange(SPAN, dtype=jnp.int32)[:, None], 0), axis=0
    )
    visible = jnp.arange(page, dtype=jnp.int32)[None, None, :] < seen[:, :, None]
    mask = visible.reshape(SPAN, slots * page).astype(jnp.bfloat16)
    mask_rows = jnp.concatenate([mask, jnp.zeros((16 - SPAN, slots * page), jnp.bfloat16)], axis=0)
    mask_each = jnp.broadcast_to(mask[:, None, :], (SPAN, 16, slots * page))

    vmem = pl.BlockSpec(memory_space=pltpu.VMEM)
    anywhere = pl.BlockSpec(memory_space=pl.ANY)
    dma = pltpu.SemaphoreType.DMA
    n_rows = GROUP * tokens
    bf16, f32 = jnp.bfloat16, jnp.float32
    scratch = [pltpu.VMEM((SPAN, tokens, WIDE), bf16) for _ in range(heads)] + [
        pltpu.VMEM((tokens, cols), bf16),
        pltpu.VMEM((tokens, cols), bf16),
        pltpu.VMEM((heads, slots, page, HEAD_SIZE), bf16),
        pltpu.VMEM((heads, slots, page, HEAD_SIZE), bf16),
        pltpu.VMEM((n_rows, slots * page), bf16),
        pltpu.VMEM((heads, n_rows, HEAD_SIZE), f32),
        pltpu.VMEM((heads, 16, n_rows), f32),
        pltpu.VMEM((heads, SPAN - 1, tokens, WIDE), bf16),
        pltpu.VMEM((heads, 16, n_rows), f32),
        pltpu.VMEM((heads, SPAN - 1, tokens, WIDE), bf16),
        pltpu.VMEM((heads, SPAN - 1, 16, n_rows), f32),
        pltpu.VMEM((heads, tokens, WIDE), bf16),
        dma((heads, 2)),
        dma((2 * heads + 2,)),
        dma((heads, n_tensor)),
        dma((heads, n_tensor)),
        dma((2, n_tensor)),
        dma((2, n_tensor)),
        dma((heads, SPAN)),
        dma((heads, SPAN)),
        dma((heads, SPAN)),
        dma((heads, SPAN)),
        dma((heads, SPAN)),
        dma((heads, SPAN)),
        dma((heads, n_tensor)),
        dma((heads, n_tensor)),
    ]
    return pl.pallas_call(
        functools.partial(kernel, n_pool, n_tensor, heads),
        out_shape=jax.ShapeDtypeStruct(queries.shape, queries.dtype),
        in_specs=[pl.BlockSpec(memory_space=pltpu.SMEM), vmem, vmem] + [anywhere] * 5,
        out_specs=anywhere,
        scratch_shapes=scratch,
        cost_estimate=pl.CostEstimate(
            flops=12 * heads * n_rows * slots * page * HEAD_SIZE,
            bytes_accessed=4 * slots * page * cols,
            transcendentals=2 * heads * n_rows * slots * page,
        ),
        compiler_params=pltpu.CompilerParams(
            collective_id=0, has_side_effects=True, vmem_limit_bytes=48 * 1024 * 1024
        ),
    )(
        distance,
        mask_rows,
        mask_each,
        queries,
        incoming_keys,
        incoming_values,
        k_pages,
        v_pages,
    )


def solution(mesh):
    placed = (
        P(("pool", "tensor"), None),
        P(("pool", "tensor"), None),
        P(("pool", "tensor"), None),
        P("pool", None, "tensor"),
        P("pool", None, "tensor"),
        P(),
        P(),
    )
    return jax.shard_map(
        functools.partial(on_device, mesh.shape["pool"], mesh.shape["tensor"]),
        mesh=mesh,
        in_specs=placed,
        out_specs=P(("pool", "tensor"), None),
        check_vma=False,
    )
```

time: 257 us -> 83.7 us (0.33)
  Pallas kernels: 0 us -> 74.9 us
  waiting for transfers between devices: 74.8 us -> 0 us
  local copies, waits for them, and re-layouts: 79.7 us -> 7.89 us
  matrix products: 66 us -> 0 us
  starting transfers between devices: 18.2 us -> 0 us
  blocking collectives: 12.1 us -> 0 us
  other arithmetic: 5.12 us -> 0.6 us
    pallas_call x0 -> x1, Pallas kernels: none -> 74.9 us  [on_device(): pl.pallas_call(functools.partial(kernel, n_pool, n_tensor, heads), out_sh...]
    ppermute x9 -> x0, waiting for transfers between devices: 68.2 us -> none  [shifted(): return lax.ppermute(block, axis, route)]
    dot_general x18 -> x0, matrix products: 66 us -> none  [the longest x4 47.6 us: compute(): jnp.einsum('pd,pqx->dqx', hot_block, numerator, precision=lax.Precision.H...]
    reshape x10 -> x0, local copies, waits for them, and re-layouts: 22.9 us -> none  [the longest x4 21.9 us: compute(): numerator.reshape(group_pages, stretch_len, head_count * HEAD_SIZE)]
    gather x9 -> x1, local copies, waits for them, and re-layouts: 20.9 us -> 1.3 us  [on_device(): jnp.take(lengths, owners)[:, None, None] - page_index * page]
    all_to_all x1 -> x0, blocking collectives: 12.1 us -> none  [on_device(): lax.all_to_all(attended, 'tensor', split_axis=0, concat_axis=1, tiled=True)]
    all_to_all x3 -> x0, starting transfers between devices: 11.1 us -> none  [the longest x1 4.21 us: on_device(): lax.all_to_all(queries, 'tensor', split_axis=1, concat_axis=0, tiled=True)]
    dynamic_slice x4 -> x0, local copies, waits for them, and re-layouts: 7.34 us -> none  [on_device(): (numer_acc, total_acc), _ = lax.scan(one_group, start_offset, input_arrays)]
  transfers between devices with their start and end apart: 12 -> 0, of which waited for: 5 -> 0; matrix products, arithmetic and copies ran while one was open for 56% -> 0% of each run, Pallas kernels for 0% -> 0%
where the time goes in v1:
time: 83.7 us; the launch traced here: 83.4 us
  Pallas kernels  74.9 us (89%)
  local copies, waits for them, and re-layouts  7.89 us (9%)
    pallas_call x1, Pallas kernels, on_device(): pl.pallas_call(functools.partial(kernel, n_pool, n_tensor, heads), out_sh...  74.9 us
    unnamed x12, local copies, waits for them, and re-layouts  5.99 us

profile of v1, /device:TPU:0, one launch (start us, length us, event | category | flops | bytes accessed | tf_op | source)
XLA Modules:
  0.0 83.4 jit_solution(9242267514507961348)
XLA Ops:
  0.0 0.0 copy-start
  0.1 1.3 %gather_fusion.1 = s32[4]{0:T(128)S(1)} fusion(s32[16]{0:T(128)} %param.13, s32[1024]{0:T(1024)S(1)} %pad_clamp_fusion), kind=kCustom, calls=%fused_computation.1 | custom fusion | bytes 48 | tf_op jit(solution)/shard_map/jit(_take)/gather | solution.py:331
  1.4 0.0 copy-done
  1.4 0.6 gather_fusion
  1.9 0.1 broadcast_subtract_fusion
  2.0 0.2 fusion
  2.2 0.2 compare_reduce_fusion
  2.5 0.1 broadcast_bitcast_fusion
  2.6 0.0 copy-start.1
  2.6 2.2 %copy-done.1 = bf16[16,128,1024]{2,1,0:T(8,128)(2,1)S(1)} copy-done((bf16[16,128,1024]{2,1,0:T(8,128)(2,1)S(1)}, bf16[16,128,1024]{2,1,0:T(8,128)(2,1)}, u32[]{:S(2)}) %copy-start.1) | copy-done | bytes 4194328
  4.8 0.0 copy-start.2
  4.8 1.0 %copy-done.2 = bf16[64,4096]{1,0:T(8,128)(2,1)S(1)} copy-done((bf16[64,4096]{1,0:T(8,128)(2,1)S(1)}, bf16[64,4096]{1,0:T(8,128)(2,1)}, u32[]{:S(2)}) %copy-start.2) | copy-done | bytes 524312
  5.9 0.0 copy-start.3
  5.9 0.9 %copy-done.3 = bf16[64,2048]{1,0:T(8,128)(2,1)S(1)} copy-done((bf16[64,2048]{1,0:T(8,128)(2,1)S(1)}, bf16[64,2048]{1,0:T(8,128)(2,1)}, u32[]{:S(2)}) %copy-start.3) | copy-done | bytes 262168
  6.8 0.0 copy-start.4
  6.8 0.9 %copy-done.4 = bf16[64,2048]{1,0:T(8,128)(2,1)S(1)} copy-done((bf16[64,2048]{1,0:T(8,128)(2,1)S(1)}, bf16[64,2048]{1,0:T(8,128)(2,1)}, u32[]{:S(2)}) %copy-start.4) | copy-done | bytes 262168
  7.8 74.9 %shard_map.73 = bf16[64,4096]{1,0:T(8,128)(2,1)S(1)} custom-call(s32[16]{0:T(128)S(1)} %select_reduce_fusion.dist, bf16[16,2048]{1,0:T(8,128)(2,1)S(1)} %concatenate.3.mask_rows, bf16[4,16,2048]{2,1,0:T(8,128)(2,1)S(1)} %broadcast_in_dim.56.mask_each, bf16[64,4096]{1,0:T(8,128)(2,1)S(1)} %copy-done.2, bf16[64,2048]{1,0:T(8,128)(2,1)S(1)} %copy-done.3, ...), custom_call_target="tpu_custom_call" | custom-call | flops 6442450944 | bytes 8388608 | tf_op jit(solution)/shard_map/pallas_call | solution.py:374
  82.6 0.8 copy.13
  (11 shorter events, 0.1 us)
Async XLA Ops:
  0.0 1.4 %copy-start = (s32[16,64]{1,0:T(8,128)S(1)}, s32[16,64]{1,0:T(8,128)}, u32[]{:S(2)}) copy-start(s32[16,64]{1,0:T(8,128)} %param.12) | copy-start | bytes 12292
  2.6 2.2 %copy-start.1 = (bf16[16,128,1024]{2,1,0:T(8,128)(2,1)S(1)}, bf16[16,128,1024]{2,1,0:T(8,128)(2,1)}, u32[]{:S(2)}) copy-start(bf16[16,128,1024]{2,1,0:T(8,128)(2,1)} %k_pages.1) | copy-start | bytes 12582916
  4.8 1.0 %copy-start.2 = (bf16[64,4096]{1,0:T(8,128)(2,1)S(1)}, bf16[64,4096]{1,0:T(8,128)(2,1)}, u32[]{:S(2)}) copy-start(bf16[64,4096]{1,0:T(8,128)(2,1)} %q_in.1) | copy-start | bytes 1572868
  5.9 0.9 %copy-start.3 = (bf16[64,2048]{1,0:T(8,128)(2,1)S(1)}, bf16[64,2048]{1,0:T(8,128)(2,1)}, u32[]{:S(2)}) copy-start(bf16[64,2048]{1,0:T(8,128)(2,1)} %k_in.1) | copy-start | bytes 786436
  6.8 0.9 %copy-start.4 = (bf16[64,2048]{1,0:T(8,128)(2,1)S(1)}, bf16[64,2048]{1,0:T(8,128)(2,1)}, u32[]{:S(2)}) copy-start(bf16[64,2048]{1,0:T(8,128)(2,1)} %v_in.1) | copy-start | bytes 786436

commit v2 on v1

--- a/solution.py
+++ b/solution.py
@@ -65,6 +65,8 @@
         total_out,
         numer_in,
         total_in,
+        kept_numer,
+        relay_in,
         done,
         page_sem,
         local_sem,
@@ -182,32 +184,77 @@
         for c in pair:
             c.start()
 
-    forward = []
+    even = lax.rem(p, 2) == 0
+
+    def pass_query(h, have, give, hop, sem):
+        return remote(
+            qbufs[h].at[have],
+            qbufs[h].at[give],
+            qf_send.at[h, sem],
+            qf_recv.at[h, give],
+            pool_at(hop),
+        )
+
     for h in range(heads):
         local[h].wait()
         for c in exchange[h]:
             c.wait_recv()
-        forward.append(
-            [
-                remote(
-                    qbufs[h].at[0],
-                    qbufs[h].at[d],
-                    qf_send.at[h, d],
-                    qf_recv.at[h, d],
-                    pool_at(d),
-                )
-                for d in range(1, SPAN)
-            ]
-        )
-        for c in forward[h]:
-            c.start()
-
-    back = []
+
+        @pl.when(even)
+        def _():
+            pass_query(h, 0, 2, 2, 1).start()
+            pass_query(h, 0, 1, 1, 0).start()
+
+        @pl.when(jnp.logical_not(even))
+        def _():
+            pass_query(h, 0, 1, 1, 0).start()
+            pass_query(h, 0, 3, 3, 1).start()
+
+    def send_numer(h, d, dst, recv, hop, sem):
+        return remote(
+            numer_out.at[h, d - 1], dst, nr_send.at[h, sem], nr_recv.at[h, recv], pool_at(hop)
+        )
+
+    def from_even(h):
+        return [
+            send_numer(h, 3, numer_in.at[h, 1], 1, -3, 0),
+            send_numer(h, 1, numer_in.at[h, 0], 0, -1, 1),
+            send_numer(h, 2, numer_in.at[h, 1], 1, -2, 2),
+        ]
+
+    def from_odd(h):
+        return [
+            send_numer(h, 1, numer_in.at[h, 0], 0, -1, 0),
+            send_numer(h, 2, relay_in.at[h, 0], 2, -1, 1),
+            send_numer(h, 3, relay_in.at[h, 1], 3, -1, 2),
+        ]
+
+    def combine(h):
+        @pl.when(even)
+        def _():
+            for d in (1, 2):
+                from_odd(h)[d].wait_recv()
+                both = kept_numer[h, d - 1] + rows_by_head(relay_in[h, d - 1].astype(jnp.float32))
+                numer_out[h, d - 1] = tokens_by_head(both.astype(jnp.bfloat16))
+                from_even(h)[d].start()
+
+    totals_back = []
     for h in range(heads):
         for c in page_copies[h]:
             c.wait()
-        for c in forward[h]:
-            c.wait_recv()
+        pass_query(h, 0, 1, 1, 0).wait_recv()
+
+        @pl.when(even)
+        def _():
+            pass_query(h, 1, 2, 1, 2).start()
+
+        pass_query(h, 0, 2, 2, 0).wait_recv()
+
+        @pl.when(even)
+        def _():
+            pass_query(h, 2, 3, 1, 3).start()
+
+        pass_query(h, 0, 3, 3, 0).wait_recv()
 
         qbuf = qbufs[h]
 
@@ -225,11 +272,21 @@
             weights[...],
             (((1,), (1,)), ((), ())),
             preferred_element_type=jnp.float32,
-        )
+        )[:8]
         own_total[h] = totals
         total_out[h] = totals
-        back.append([])
-        for d in list(range(1, SPAN)) + [0]:
+        totals_back.append([])
+        for d in range(1, SPAN):
+            c = remote(
+                total_out.at[h],
+                total_in.at[h, d - 1],
+                tr_send.at[h, d],
+                tr_recv.at[h, d],
+                pool_at(-d),
+            )
+            c.start()
+            totals_back[h].append(c)
+        for d in (3, 2, 1, 0):
             all_weights = weights[...]
             kept = all_weights.reshape(-1, 16, slots * page) * mask_each[d][None]
             numer = jnp.dot(
@@ -237,27 +294,30 @@
             )
             if d == 0:
                 own_numer[h] = numer
+                continue
+            if d == 3:
+                numer_out[h, d - 1] = tokens_by_head(numer.astype(jnp.bfloat16))
+
+                @pl.when(even)
+                def _():
+                    from_even(h)[0].start()
+
             else:
-                numer_out[h, d - 1] = tokens_by_head(numer.astype(jnp.bfloat16))
-                pair = [
-                    remote(
-                        numer_out.at[h, d - 1],
-                        numer_in.at[h, d - 1],
-                        nr_send.at[h, d],
-                        nr_recv.at[h, d],
-                        pool_at(-d),
-                    ),
-                    remote(
-                        total_out.at[h],
-                        total_in.at[h, d - 1],
-                        tr_send.at[h, d],
-                        tr_recv.at[h, d],
-                        pool_at(-d),
-                    ),
-                ]
-                for c in pair:
-                    c.start()
-                back[h] += pair
+
+                @pl.when(even)
+                def _():
+                    kept_numer[h, d - 1] = numer
+
+                @pl.when(jnp.logical_not(even))
+                def _():
+                    numer_out[h, d - 1] = tokens_by_head(numer.astype(jnp.bfloat16))
+
+            @pl.when(jnp.logical_not(even))
+            def _():
+                from_odd(h)[d - 1].start()
+
+        if h > 0:
+            combine(h - 1)
 
     for c in local_kv:
         c.wait()
@@ -274,17 +334,22 @@
         own_numer[h] += jnp.dot(fresh, v_own[:, cols], preferred_element_type=jnp.float32)
         own_total[h] += lax.dot_general(
             ones, fresh, (((1,), (1,)), ((), ())), preferred_element_type=jnp.float32
-        )
+        )[:8]
+
+    combine(heads - 1)
 
     finished = []
     for h in range(heads):
-        for c in back[h]:
+        for c in totals_back[h]:
             c.wait_recv()
+        send_numer(h, 1, numer_in.at[h, 0], 0, -1, 0).wait_recv()
+        send_numer(h, 1, numer_in.at[h, 1], 1, -2, 0).wait_recv()
         total = own_total[h, 0:1, :]
         numer = own_numer[h]
         for d in range(1, SPAN):
             total = total + total_in[h, d - 1, d : d + 1, :]
-            numer = numer + rows_by_head(numer_in[h, d - 1].astype(jnp.float32))
+        for d in range(2):
+            numer = numer + rows_by_head(numer_in[h, d].astype(jnp.float32))
         per_row = jnp.broadcast_to(total, (128, n_rows)).T
         per_row = jnp.concatenate([per_row] * (HEAD_SIZE // 128), axis=1)
         done[h] = tokens_by_head((numer / per_row).astype(jnp.bfloat16))
@@ -306,8 +371,25 @@
             finished[h].append(c)
 
     for h in range(heads):
-        for c in exchange[h] + forward[h] + back[h]:
+        for c in exchange[h] + totals_back[h]:
             c.wait_send()
+
+        @pl.when(even)
+        def _():
+            pass_query(h, 0, 1, 1, 0).wait_send()
+            pass_query(h, 0, 2, 2, 1).wait_send()
+            pass_query(h, 1, 2, 1, 2).wait_send()
+            pass_query(h, 2, 3, 1, 3).wait_send()
+            for c in from_even(h):
+                c.wait_send()
+
+        @pl.when(jnp.logical_not(even))
+        def _():
+            pass_query(h, 0, 1, 1, 0).wait_send()
+            pass_query(h, 0, 3, 3, 1).wait_send()
+            for c in from_odd(h):
+                c.wait_send()
+
         for c in finished[h]:
             c.wait()
     for c in exchange_kv:
@@ -322,13 +404,18 @@
     rows = queries.shape[0]
     tokens = rows * n_tensor
     holder = lax.axis_index("pool")
-    owners = (holder - jnp.arange(SPAN, dtype=jnp.int32)) % n_pool
-    table_rows = jnp.take(page_table, owners, axis=0)
+    first = holder - (SPAN - 1) + n_pool
+
+    def of_owners(whole):
+        twice = jnp.concatenate([whole, whole], axis=0)
+        return lax.dynamic_slice_in_dim(twice, first, SPAN, axis=0)[::-1]
+
+    table_rows = of_owners(page_table)
     global_slot = holder * slots + jnp.arange(slots, dtype=jnp.int32)
     matches = table_rows[:, :, None] == global_slot[None, None, :]
     page_index = jnp.arange(table_rows.shape[1], dtype=jnp.int32)[None, :, None]
     seen = jnp.sum(
-        jnp.where(matches, jnp.take(lengths, owners)[:, None, None] - page_index * page, 0), axis=1
+        jnp.where(matches, of_owners(lengths)[:, None, None] - page_index * page, 0), axis=1
     )
     distance = jnp.sum(
         jnp.where(jnp.any(matches, axis=1), jnp.arange(SPAN, dtype=jnp.int32)[:, None], 0), axis=0
@@ -339,7 +426,7 @@
     mask_each = jnp.broadcast_to(mask[:, None, :], (SPAN, 16, slots * page))
 
     vmem = pl.BlockSpec(memory_space=pltpu.VMEM)
-    anywhere = pl.BlockSpec(memory_space=pl.ANY)
+    anywhere = pl.BlockSpec(memory_space=pltpu.HBM)
     dma = pltpu.SemaphoreType.DMA
     n_rows = GROUP * tokens
     bf16, f32 = jnp.bfloat16, jnp.float32
@@ -350,11 +437,13 @@
         pltpu.VMEM((heads, slots, page, HEAD_SIZE), bf16),
         pltpu.VMEM((n_rows, slots * page), bf16),
         pltpu.VMEM((heads, n_rows, HEAD_SIZE), f32),
-        pltpu.VMEM((heads, 16, n_rows), f32),
+        pltpu.VMEM((heads, 8, n_rows), f32),
         pltpu.VMEM((heads, SPAN - 1, tokens, WIDE), bf16),
-        pltpu.VMEM((heads, 16, n_rows), f32),
-        pltpu.VMEM((heads, SPAN - 1, tokens, WIDE), bf16),
-        pltpu.VMEM((heads, SPAN - 1, 16, n_rows), f32),
+        pltpu.VMEM((heads, 8, n_rows), f32),
+        pltpu.VMEM((heads, 2, tokens, WIDE), bf16),
+        pltpu.VMEM((heads, SPAN - 1, 8, n_rows), f32),
+        pltpu.VMEM((heads, 2, n_rows, HEAD_SIZE), f32),
+        pltpu.VMEM((heads, 2, tokens, WIDE), bf16),
         pltpu.VMEM((heads, tokens, WIDE), bf16),
         dma((heads, 2)),
         dma((2 * heads + 2,)),
@@ -383,7 +472,7 @@
             transcendentals=2 * heads * n_rows * slots * page,
         ),
         compiler_params=pltpu.CompilerParams(
-            collective_id=0, has_side_effects=True, vmem_limit_bytes=48 * 1024 * 1024
+            collective_id=0, has_side_effects=True, vmem_limit_bytes=62 * 1024 * 1024
         ),
     )(
         distance,

time: 83.7 us -> 54.8 us (0.65)
  Pallas kernels: 74.9 us -> 48.5 us
  local copies, waits for them, and re-layouts: 7.89 us -> 3.5 us
  other arithmetic: 0.6 us -> 2.58 us
    pallas_call x1, Pallas kernels: 74.9 us -> 48.5 us  [on_device(): pl.pallas_call(functools.partial(kernel, n_pool, n_tensor, heads), out_sh...]
    unnamed x12 -> x2, local copies, waits for them, and re-layouts: 5.99 us -> 1.94 us
    gather x2 -> x0, local copies, waits for them, and re-layouts: 1.86 us -> none  [the longest x1 1.3 us: on_device(): jnp.take(lengths, owners)[:, None, None] - page_index * page]
    concatenate x0 -> x2, other arithmetic: none -> 1.52 us  [of_owners(): twice = jnp.concatenate([whole, whole], axis=0)]
where the time goes in v2:
time: 54.8 us; the launch traced here: 54.6 us
  Pallas kernels  48.5 us (89%)
  local copies, waits for them, and re-layouts  3.5 us (6%)
  other arithmetic  2.58 us (5%)
    pallas_call x1, Pallas kernels, on_device(): pl.pallas_call(functools.partial(kernel, n_pool, n_tensor, heads), out_sh...  48.5 us
    unnamed x2, local copies, waits for them, and re-layouts  1.94 us
    concatenate x2, other arithmetic, of_owners(): twice = jnp.concatenate([whole, whole], axis=0)  1.52 us

profile of v2, /device:TPU:0, one launch (start us, length us, event | category | flops | bytes accessed | tf_op | source)
XLA Modules:
  0.0 54.6 jit_solution(8625596866291414035)
XLA Ops:
  0.0 0.8 %pad_add_fusion = s32[32]{0:T(128)S(1)} fusion(s32[16]{0:T(128)} %param.13), kind=kLoop, calls=%fused_computation.12 | loop fusion | flops 32 | bytes 192 | tf_op jit(solution)/shard_map/concatenate | solution.py:410
  0.8 0.1 dynamic_slice.7
  0.9 0.1 rev.7
  1.0 0.1 broadcast_subtract_fusion
  1.1 0.7 %fusion.2 = s32[4,64]{1,0:T(4,128)S(1)} fusion(s32[]{:T(128)S(6)} %select_n.12, s32[16,64]{1,0:T(8,128)} %param.12), kind=kLoop, calls=%fused_computation.9 | loop fusion | flops 256 | bytes 5124 | tf_op jit(solution)/shard_map/concatenate | solution.py:410
  1.8 0.2 fusion
  2.0 0.2 compare_reduce_fusion
  2.2 0.5 select_reduce_fusion.dist
  2.8 0.1 broadcast_bitcast_fusion
  2.9 0.6 %concatenate.11.mask_rows = bf16[16,2048]{1,0:T(8,128)(2,1)} pad(bf16[4,2048]{1,0:T(4,128)(2,1)S(1)} %fusion.1, bf16[]{:T(256)} %constant.23.clone.1), padding=0_12x0_0 | pad | bytes 81922 | tf_op jit(solution)/shard_map/concatenate | solution.py:425
  3.5 0.7 %broadcast_in_dim.42.mask_each = bf16[4,16,2048]{2,1,0:T(8,128)(2,1)} broadcast(bf16[4,2048]{1,0:T(4,128)(2,1)S(1)} %fusion.1), dimensions={0,2} | broadcast | bytes 278528 | tf_op jit(solution)/shard_map/broadcast_in_dim | solution.py:426
  4.2 48.5 %shard_map.73 = bf16[64,4096]{1,0:T(8,128)(2,1)} custom-call(s32[16]{0:T(128)} %select_reduce_fusion.dist, bf16[16,2048]{1,0:T(8,128)(2,1)} %concatenate.11.mask_rows, bf16[4,16,2048]{2,1,0:T(8,128)(2,1)} %broadcast_in_dim.42.mask_each, bf16[64,4096]{1,0:T(8,128)(2,1)} %q_in.1, bf16[64,2048]{1,0:T(8,128)(2,1)} %k_in.1, bf16[64,2048]{1,0:T(8,128)(2,1)} %v_in.1, ...), custom_call_target="tpu_custom_call" | custom-call | flops 6442450944 | bytes 8388608 | tf_op jit(solution)/shard_map/pallas_call | solution.py:463
  52.7 1.9 %copy.13 = bf16[64,4096]{1,0:T(8,128)(2,1)} copy(bf16[64,4096]{1,0:T(8,128)(2,1)} %shard_map.73) | data formatting | bytes 1048576
  (5 shorter events, 0.1 us)

commit v3 on v2

--- a/solution.py
+++ b/solution.py
@@ -41,9 +41,7 @@
     n_pool,
     n_tensor,
     heads,
-    dist,
-    mask_rows,
-    mask_each,
+    seen_all,
     q_in,
     k_in,
     v_in,
@@ -54,6 +52,8 @@
 ):
     qbufs = scratch[:heads]
     (
+        mask_rows,
+        mask_each,
         k_own,
         v_own,
         k_mem,
@@ -238,6 +238,22 @@
                 numer_out[h, d - 1] = tokens_by_head(both.astype(jnp.bfloat16))
                 from_even(h)[d].start()
 
+    seen = [[seen_all[lax.rem(p - d + n_pool, n_pool), s] for s in range(slots)] for d in range(SPAN)]
+    dist = [
+        sum(jnp.where(seen[d][s] > 0, d, 0).astype(jnp.int32) for d in range(1, SPAN))
+        for s in range(slots)
+    ]
+    tile = (16, page)
+    column = lax.broadcasted_iota(jnp.int32, tile, 1)
+    row = lax.broadcasted_iota(jnp.int32, tile, 0)
+    for s in range(slots):
+        cols = slice(s * page, (s + 1) * page)
+        by_row = jnp.zeros(tile, jnp.int32)
+        for d in range(SPAN):
+            mask_each[d, :, cols] = jnp.where(column < seen[d][s], 1.0, 0.0).astype(jnp.bfloat16)
+            by_row = jnp.where(row == d, seen[d][s], by_row)
+        mask_rows[:, cols] = jnp.where(column < by_row, 1.0, 0.0).astype(jnp.bfloat16)
+
     totals_back = []
     for h in range(heads):
         for c in page_copies[h]:
@@ -258,13 +274,10 @@
 
         qbuf = qbufs[h]
 
-        @pl.loop(0, slots // 4)
-        def _(j):
-            for u in range(4):
-                s = j * 4 + u
-                query = rows_by_head(qbuf[dist[s]])
-                cols = pl.ds(pl.multiple_of(s * page, page), page)
-                weights[:, cols] = weigh(query, k_mem[h, s]).astype(jnp.bfloat16)
+        for s in range(slots):
+            query = rows_by_head(qbuf[dist[s]])
+            cols = slice(s * page, (s + 1) * page)
+            weights[:, cols] = weigh(query, k_mem[h, s]).astype(jnp.bfloat16)
 
         values = v_mem[h].reshape(slots * page, HEAD_SIZE)
         totals = lax.dot_general(
@@ -404,33 +417,18 @@
     rows = queries.shape[0]
     tokens = rows * n_tensor
     holder = lax.axis_index("pool")
-    first = holder - (SPAN - 1) + n_pool
-
-    def of_owners(whole):
-        twice = jnp.concatenate([whole, whole], axis=0)
-        return lax.dynamic_slice_in_dim(twice, first, SPAN, axis=0)[::-1]
-
-    table_rows = of_owners(page_table)
     global_slot = holder * slots + jnp.arange(slots, dtype=jnp.int32)
-    matches = table_rows[:, :, None] == global_slot[None, None, :]
-    page_index = jnp.arange(table_rows.shape[1], dtype=jnp.int32)[None, :, None]
-    seen = jnp.sum(
-        jnp.where(matches, of_owners(lengths)[:, None, None] - page_index * page, 0), axis=1
-    )
-    distance = jnp.sum(
-        jnp.where(jnp.any(matches, axis=1), jnp.arange(SPAN, dtype=jnp.int32)[:, None], 0), axis=0
-    )
-    visible = jnp.arange(page, dtype=jnp.int32)[None, None, :] < seen[:, :, None]
-    mask = visible.reshape(SPAN, slots * page).astype(jnp.bfloat16)
-    mask_rows = jnp.concatenate([mask, jnp.zeros((16 - SPAN, slots * page), jnp.bfloat16)], axis=0)
-    mask_each = jnp.broadcast_to(mask[:, None, :], (SPAN, 16, slots * page))
-
-    vmem = pl.BlockSpec(memory_space=pltpu.VMEM)
+    matches = page_table[:, :, None] == global_slot[None, None, :]
+    page_index = jnp.arange(page_table.shape[1], dtype=jnp.int32)[None, :, None]
+    seen_all = jnp.sum(jnp.where(matches, lengths[:, None, None] - page_index * page, 0), axis=1)
+
     anywhere = pl.BlockSpec(memory_space=pltpu.HBM)
     dma = pltpu.SemaphoreType.DMA
     n_rows = GROUP * tokens
     bf16, f32 = jnp.bfloat16, jnp.float32
     scratch = [pltpu.VMEM((SPAN, tokens, WIDE), bf16) for _ in range(heads)] + [
+        pltpu.VMEM((16, slots * page), bf16),
+        pltpu.VMEM((SPAN, 16, slots * page), bf16),
         pltpu.VMEM((tokens, cols), bf16),
         pltpu.VMEM((tokens, cols), bf16),
         pltpu.VMEM((heads, slots, page, HEAD_SIZE), bf16),
@@ -463,8 +461,8 @@
     return pl.pallas_call(
         functools.partial(kernel, n_pool, n_tensor, heads),
         out_shape=jax.ShapeDtypeStruct(queries.shape, queries.dtype),
-        in_specs=[pl.BlockSpec(memory_space=pltpu.SMEM), vmem, vmem] + [anywhere] * 5,
-        out_specs=anywhere,
+        in_specs=[pl.BlockSpec(memory_space=pltpu.SMEM)] + [anywhere] * 5,
+        out_specs=pl.BlockSpec(memory_space=pl.ANY),
         scratch_shapes=scratch,
         cost_estimate=pl.CostEstimate(
             flops=12 * heads * n_rows * slots * page * HEAD_SIZE,
@@ -475,9 +473,7 @@
             collective_id=0, has_side_effects=True, vmem_limit_bytes=62 * 1024 * 1024
         ),
     )(
-        distance,
-        mask_rows,
-        mask_each,
+        seen_all,
         queries,
         incoming_keys,
         incoming_values,

time: 54.8 us -> 52.4 us (0.956)
  local copies, waits for them, and re-layouts: 3.5 us -> 1.87 us
  Pallas kernels: 48.5 us -> 47.8 us
    concatenate x2 -> x0, other arithmetic: 1.52 us -> none  [of_owners(): twice = jnp.concatenate([whole, whole], axis=0)]
    reduce_sum x2 -> x1, other arithmetic: 0.74 us -> 1.71 us  [on_device(): jnp.sum(jnp.where(matches, lengths[:, None, None] - page_index * page, 0)...]
    broadcast_in_dim x1 -> x0, local copies, waits for them, and re-layouts: 0.72 us -> none  [on_device(): mask_each = jnp.broadcast_to(mask[:, None, :], (SPAN, 16, slots * page))]
    pallas_call x1, Pallas kernels: 48.5 us -> 47.8 us  [on_device(): pl.pallas_call(functools.partial(kernel, n_pool, n_tensor, heads), out_sh...]
    sub x1, other arithmetic: 0.07 us -> 0.72 us  [on_device(): lengths[:, None, None] - page_index * page]
    concatenate x1 -> x0, local copies, waits for them, and re-layouts: 0.63 us -> none  [on_device(): jnp.concatenate([mask, jnp.zeros((16 - SPAN, slots * page), jnp.bfloat16)...]
    unnamed x2 -> x1, local copies, waits for them, and re-layouts: 1.94 us -> 1.87 us
where the time goes in v3:
time: 52.4 us; the launch traced here: 52.1 us
  Pallas kernels  47.8 us (91%)
  other arithmetic  2.44 us (5%)
  local copies, waits for them, and re-layouts  1.87 us (4%)
    pallas_call x1, Pallas kernels, on_device(): pl.pallas_call(functools.partial(kernel, n_pool, n_tensor, heads), out_sh...  47.8 us
    unnamed x1, local copies, waits for them, and re-layouts  1.87 us
    reduce_sum x1, other arithmetic, on_device(): jnp.sum(jnp.where(matches, lengths[:, None, None] - page_index * page, 0)...  1.71 us

profile of v3, /device:TPU:0, one launch (start us, length us, event | category | flops | bytes accessed | tf_op | source)
XLA Modules:
  0.0 52.1 jit_solution(5689604742501648220)
XLA Ops:
  0.0 0.7 %broadcast_subtract_fusion = s32[16,64]{1,0:T(8,128)S(1)} fusion(s32[64]{0:T(128)S(1)} %iota_multiply_fusion, s32[16]{0:T(128)} %param.13), kind=kLoop, calls=%fused_computation.1 | loop fusion | flops 1024 | bytes 4416 | tf_op jit(solution)/shard_map/sub | solution.py:423
  0.7 1.7 %select_reduce_fusion.seen_all = s32[16,16]{1,0:T(8,128)} fusion(s32[16,64]{1,0:T(8,128)S(1)} %broadcast_subtract_fusion, s32[16,64]{1,0:T(8,128)} %param.12, s32[16]{0:T(128)S(1)} %iota_add_fusion), kind=kLoop, calls=%fused_computation | loop fusion | flops 48896 | bytes 9280 | tf_op jit(solution)/shard_map/reduce_sum | solution.py:423
  2.4 47.8 %shard_map.73 = bf16[64,4096]{1,0:T(8,128)(2,1)} custom-call(s32[16,16]{1,0:T(8,128)} %select_reduce_fusion.seen_all, bf16[64,4096]{1,0:T(8,128)(2,1)} %q_in.1, bf16[64,2048]{1,0:T(8,128)(2,1)} %k_in.1, bf16[64,2048]{1,0:T(8,128)(2,1)} %v_in.1, bf16[16,128,1024]{2,1,0:T(8,128)(2,1)} %k_pages.1, bf16[16,128,1024]{2,1,0:T(8,128)(2,1)} %v_pages.1), custom_call_target="tpu_custom_call" | custom-call | flops 6442450944 | bytes 8388608 | tf_op jit(solution)/shard_map/pallas_call | solution.py:461
  50.2 1.9 %copy.9 = bf16[64,4096]{1,0:T(8,128)(2,1)} copy(bf16[64,4096]{1,0:T(8,128)(2,1)} %shard_map.73) | data formatting | bytes 1048576
  (2 shorter events, 0.0 us)

commit v4 on v3

--- a/solution.py
+++ b/solution.py
@@ -176,10 +176,6 @@
                     (p, tensor_at(i)),
                 )
             )
-    for c in local_kv:
-        c.start()
-    for c in exchange_kv:
-        c.start()
     for pair in page_copies[1:]:
         for c in pair:
             c.start()
@@ -209,6 +205,11 @@
         def _():
             pass_query(h, 0, 1, 1, 0).start()
             pass_query(h, 0, 3, 3, 1).start()
+
+    for c in local_kv:
+        c.start()
+    for c in exchange_kv:
+        c.start()
 
     def send_numer(h, d, dst, recv, hop, sem):
         return remote(

time: 52.4 us -> 52.4 us (level)
  no operation moved by 1% of the time
where the time goes in v4:
time: 52.4 us; the launch traced here: 52.1 us
  Pallas kernels  47.8 us (91%)
  other arithmetic  2.44 us (5%)
  local copies, waits for them, and re-layouts  1.87 us (4%)
    pallas_call x1, Pallas kernels, on_device(): pl.pallas_call(functools.partial(kernel, n_pool, n_tensor, heads), out_sh...  47.8 us
    unnamed x1, local copies, waits for them, and re-layouts  1.87 us
    reduce_sum x1, other arithmetic, on_device(): jnp.sum(jnp.where(matches, lengths[:, None, None] - page_index * page, 0)...  1.71 us

profile of v4, /device:TPU:0, one launch (start us, length us, event | category | flops | bytes accessed | tf_op | source)
XLA Modules:
  0.0 52.1 jit_solution(8520740267962135769)
XLA Ops:
  0.0 0.7 %broadcast_subtract_fusion = s32[16,64]{1,0:T(8,128)S(1)} fusion(s32[64]{0:T(128)S(1)} %iota_multiply_fusion, s32[16]{0:T(128)} %param.13), kind=kLoop, calls=%fused_computation.1 | loop fusion | flops 1024 | bytes 4416 | tf_op jit(solution)/shard_map/sub | solution.py:424
  0.7 1.7 %select_reduce_fusion.seen_all = s32[16,16]{1,0:T(8,128)} fusion(s32[16,64]{1,0:T(8,128)S(1)} %broadcast_subtract_fusion, s32[16,64]{1,0:T(8,128)} %param.12, s32[16]{0:T(128)S(1)} %iota_add_fusion), kind=kLoop, calls=%fused_computation | loop fusion | flops 48896 | bytes 9280 | tf_op jit(solution)/shard_map/reduce_sum | solution.py:424
  2.4 47.8 %shard_map.73 = bf16[64,4096]{1,0:T(8,128)(2,1)} custom-call(s32[16,16]{1,0:T(8,128)} %select_reduce_fusion.seen_all, bf16[64,4096]{1,0:T(8,128)(2,1)} %q_in.1, bf16[64,2048]{1,0:T(8,128)(2,1)} %k_in.1, bf16[64,2048]{1,0:T(8,128)(2,1)} %v_in.1, bf16[16,128,1024]{2,1,0:T(8,128)(2,1)} %k_pages.1, bf16[16,128,1024]{2,1,0:T(8,128)(2,1)} %v_pages.1), custom_call_target="tpu_custom_call" | custom-call | flops 6442450944 | bytes 8388608 | tf_op jit(solution)/shard_map/pallas_call | solution.py:462
  50.2 1.9 %copy.9 = bf16[64,4096]{1,0:T(8,128)(2,1)} copy(bf16[64,4096]{1,0:T(8,128)(2,1)} %shard_map.73) | data formatting | bytes 1048576
  (2 shorter events, 0.0 us)

commit v5 on v3

--- a/solution.py
+++ b/solution.py
@@ -300,11 +300,16 @@
             c.start()
             totals_back[h].append(c)
         for d in (3, 2, 1, 0):
-            all_weights = weights[...]
-            kept = all_weights.reshape(-1, 16, slots * page) * mask_each[d][None]
-            numer = jnp.dot(
-                kept.reshape(all_weights.shape), values, preferred_element_type=jnp.float32
-            )
+            if d % 2 == 1:
+                tiles = weights[...].reshape(-1, 16, slots * page)
+                kept = [
+                    (tiles * mask_each[e][None]).reshape(weights.shape) for e in (d, d - 1)
+                ]
+                two = jnp.dot(
+                    jnp.concatenate(kept, axis=0), values, preferred_element_type=jnp.float32
+                )
+            half = weights.shape[0]
+            numer = two[:half] if d % 2 == 1 else two[half:]
             if d == 0:
                 own_numer[h] = numer
                 continue

time: 52.4 us -> 52 us (level)
  no operation moved by 1% of the time
where the time goes in v5:
time: 52 us; the launch traced here: 51.7 us
  Pallas kernels  47.4 us (91%)
  other arithmetic  2.44 us (5%)
  local copies, waits for them, and re-layouts  1.87 us (4%)
    pallas_call x1, Pallas kernels, on_device(): pl.pallas_call(functools.partial(kernel, n_pool, n_tensor, heads), out_sh...  47.4 us
    unnamed x1, local copies, waits for them, and re-layouts  1.87 us
    reduce_sum x1, other arithmetic, on_device(): jnp.sum(jnp.where(matches, lengths[:, None, None] - page_index * page, 0)...  1.71 us

profile of v5, /device:TPU:0, one launch (start us, length us, event | category | flops | bytes accessed | tf_op | source)
XLA Modules:
  0.0 51.7 jit_solution(16660080231805845463)
XLA Ops:
  0.0 0.7 %broadcast_subtract_fusion = s32[16,64]{1,0:T(8,128)S(1)} fusion(s32[64]{0:T(128)S(1)} %iota_multiply_fusion, s32[16]{0:T(128)} %param.13), kind=kLoop, calls=%fused_computation.1 | loop fusion | flops 1024 | bytes 4416 | tf_op jit(solution)/shard_map/sub | solution.py:428
  0.7 1.7 %select_reduce_fusion.seen_all = s32[16,16]{1,0:T(8,128)} fusion(s32[16,64]{1,0:T(8,128)S(1)} %broadcast_subtract_fusion, s32[16,64]{1,0:T(8,128)} %param.12, s32[16]{0:T(128)S(1)} %iota_add_fusion), kind=kLoop, calls=%fused_computation | loop fusion | flops 48896 | bytes 9280 | tf_op jit(solution)/shard_map/reduce_sum | solution.py:428
  2.4 47.4 %shard_map.73 = bf16[64,4096]{1,0:T(8,128)(2,1)} custom-call(s32[16,16]{1,0:T(8,128)} %select_reduce_fusion.seen_all, bf16[64,4096]{1,0:T(8,128)(2,1)} %q_in.1, bf16[64,2048]{1,0:T(8,128)(2,1)} %k_in.1, bf16[64,2048]{1,0:T(8,128)(2,1)} %v_in.1, bf16[16,128,1024]{2,1,0:T(8,128)(2,1)} %k_pages.1, bf16[16,128,1024]{2,1,0:T(8,128)(2,1)} %v_pages.1), custom_call_target="tpu_custom_call" | custom-call | flops 6442450944 | bytes 8388608 | tf_op jit(solution)/shard_map/pallas_call | solution.py:466
  49.8 1.9 %copy.9 = bf16[64,4096]{1,0:T(8,128)(2,1)} copy(bf16[64,4096]{1,0:T(8,128)(2,1)} %shard_map.73) | data formatting | bytes 1048576
  (2 shorter events, 0.0 us)
